TPU v7x, 256 devices: a whole 4x4x8 slice. The times are simulated.
256 devices in a mesh: quad: 8 (over x, z_hi), py: 8 (over y, core), pz: 4 (over z_lo).
Axes of the slice: x: 4, y: 4, z: 8 (z_hi: 2, z_lo: 4; z = z_hi * 4 + z_lo), core: 2. Of those that a mesh axis runs over, the one named last changes fastest.
Arguments:
- source_real: float32 [4, 16, 128, 512], P(None, None, 'py', 'pz'), may hold values from -6 to 6
- source_imag: float32 [4, 16, 128, 512], P(None, None, 'py', 'pz'), may hold values from -2 to 2
- potential: float32 [16, 128, 512], P(None, 'py', 'pz'), may hold values from 0 to 2
- center: float32 [1], replicated, may hold values from 4.5 to 6
- radius: float32 [1], replicated, may hold values from 1 to 2
Outputs:
- moments: float32 [4, 2, 4, 16, 128, 512], P(None, None, None, 'quad', 'py', 'pz')
All inputs are finite; a program needn't handle non-finite values.
Results may differ from a plain program's by a relative error of at most 0.0003.
Values sent between devices are 32-bit elements; how exact they have to be, the bound alone decides.
A program may use at most 128 MiB of HBM per device.

v0:
```python
import math
import jax
import jax.numpy as jnp
from jax import lax
from jax.sharding import PartitionSpec as P

QPTS = 8
MOMS = 4
stencil_weights = (-205.0 / 72.0, 8.0 / 5.0, -1.0 / 5.0, 8.0 / 315.0, -1.0 / 560.0)


def with_halo(value, sides, width):
    edges = {}
    for axis, dim in sides:
        count, length = (lax.axis_size(axis), value.shape[dim])
        up = [(i, (i + 1) % count) for i in range(count)]
        last = lax.slice_in_dim(value, length - width, length, axis=dim)
        initial = lax.slice_in_dim(value, 0, width, axis=dim)
        edges[dim] = (
            lax.ppermute(last, axis, up),
            lax.ppermute(initial, axis, [(b, a) for a, b in up]),
        )
    done = []
    for _, dim in sides:
        low, high = edges[dim]
        around = [(width, width) if d in done else (0, 0) for d in range(value.ndim)]
        value = jnp.concatenate([jnp.pad(low, around), value, jnp.pad(high, around)], axis=dim)
        done.append(dim)
    return value


def sent_to_all(value, axis):
    count = lax.axis_size(axis)
    return lax.all_to_all(
        jnp.broadcast_to(value[None], (count, *value.shape)), axis, 0, 0, tiled=True
    )


def over_copies(value, axis):
    return sent_to_all(value, axis).sum(axis=0)


def packed_total(arrays, axis):
    ends = [0]
    for a in arrays:
        ends.append(ends[-1] + a.size)
    running = over_copies(jnp.concatenate([a.ravel() for a in arrays]), axis)
    return tuple((running[b:e].reshape(a.shape) for a, b, e in zip(arrays, ends, ends[1:])))


def apply_operator(field, potential):
    padded = with_halo(field, (("py", 4), ("pz", 5)), 4)
    width_y = field.shape[4]
    width_z = field.shape[5]
    laplace = 3.0 * stencil_weights[0] * field
    for offset in range(1, 5):
        beside_all = jnp.roll(field, offset, 3) + jnp.roll(field, -offset, 3)
        beside_all = (
            beside_all + padded[:, :, :, :, 4 + offset : 4 + offset + width_y, 4 : 4 + width_z]
        )
        beside_all = (
            beside_all + padded[:, :, :, :, 4 - offset : 4 - offset + width_y, 4 : 4 + width_z]
        )
        beside_all = (
            beside_all + padded[:, :, :, :, 4 : 4 + width_y, 4 + offset : 4 + offset + width_z]
        )
        beside_all = (
            beside_all + padded[:, :, :, :, 4 : 4 + width_y, 4 - offset : 4 - offset + width_z]
        )
        laplace = laplace + stencil_weights[offset] * beside_all
    return -0.5 * laplace + potential * field


def complex_mul(left, right):
    return (left[0] * right[0] - left[1] * right[1], left[0] * right[1] + left[1] * right[0])


def complex_div(left, right):
    norm_sq = right[0] * right[0] + right[1] * right[1]
    return (
        (left[0] * right[0] + left[1] * right[1]) / norm_sq,
        (left[1] * right[0] - left[0] * right[1]) / norm_sq,
    )


def local_bilinear(left, right):
    both = complex_mul(left, right)
    return (jnp.sum(both[0], axis=(-3, -2, -1)), jnp.sum(both[1], axis=(-3, -2, -1)))


def spread(value):
    return (value[0][..., None, None, None], value[1][..., None, None, None])


def moment_terms(solution, angles, radius_value):
    orders = jnp.arange(1, MOMS + 1).astype(jnp.float32)
    phase = orders[:, None] * angles[None, :]
    weight_re = radius_value / QPTS * jnp.cos(phase)
    weight_im = radius_value / QPTS * jnp.sin(phase)
    highest = lax.Precision.HIGHEST
    real_part = jnp.einsum("kq,qsxyz->ksxyz", weight_re, solution[:, 0], precision=highest)
    real_part = real_part - jnp.einsum(
        "kq,qsxyz->ksxyz", weight_im, solution[:, 1], precision=highest
    )
    imag_part = jnp.einsum("kq,qsxyz->ksxyz", weight_re, solution[:, 1], precision=highest)
    imag_part = imag_part + jnp.einsum(
        "kq,qsxyz->ksxyz", weight_im, solution[:, 0], precision=highest
    )
    return jnp.stack([real_part, imag_part], 1)


def per_device(source_real, source_imag, potential, center, radius):
    groups = lax.axis_size("quad")
    local_count = QPTS // groups
    first_point = lax.axis_index("quad") * local_count
    indices = (first_point + jnp.arange(local_count)).astype(jnp.float32)
    angles = 2.0 * math.pi * (indices + 0.5) / QPTS
    shift_re = center[0] + radius[0] * jnp.cos(angles)
    shift_im = radius[0] * jnp.sin(angles)
    shift_pair = (shift_re[:, None], shift_im[:, None])
    shift_field = (shift_re[:, None, None, None, None], shift_im[:, None, None, None, None])
    source = (source_real, source_imag)
    applied = apply_operator(jnp.stack(source)[None], potential)[0]
    hsource = (applied[0], applied[1])
    rho_local = local_bilinear(source, source)
    curv_local = local_bilinear(source, hsource)
    totals = packed_total((rho_local[0], rho_local[1], curv_local[0], curv_local[1]), ("py", "pz"))
    rho_first = (totals[0], totals[1])
    curv_first = (totals[2], totals[3])
    scaled = complex_mul(shift_pair, rho_first)
    denom = (scaled[0] - curv_first[0], scaled[1] - curv_first[1])
    alpha_first = complex_div(rho_first, denom)
    alpha_wide = spread(alpha_first)
    first_iterate = complex_mul(alpha_wide, source)
    shifted = complex_mul(shift_field, source)
    image = (shifted[0] - hsource[0], shifted[1] - hsource[1])
    moved = complex_mul(alpha_wide, image)
    residual = (source[0] - moved[0], source[1] - moved[1])
    hres = apply_operator(jnp.stack(residual, 1), potential)
    shifted_res = complex_mul(shift_field, residual)
    image_res = (shifted_res[0] - hres[:, 0], shifted_res[1] - hres[:, 1])
    rho_part = local_bilinear(residual, residual)
    mixed_part = local_bilinear(residual, image_res)
    paired = packed_total((rho_part[0], rho_part[1], mixed_part[0], mixed_part[1]), ("py", "pz"))
    rho_next = (paired[0], paired[1])
    mixed = (paired[2], paired[3])
    beta = complex_div(rho_next, rho_first)
    carried = complex_mul(spread(beta), source)
    direction = (residual[0] + carried[0], residual[1] + carried[1])
    correction = complex_div(complex_mul(beta, rho_next), alpha_first)
    curv_next = (mixed[0] - correction[0], mixed[1] - correction[1])
    alpha_next = complex_div(rho_next, curv_next)
    step_part = complex_mul(spread(alpha_next), direction)
    solution = jnp.stack((first_iterate[0] + step_part[0], first_iterate[1] + step_part[1]), 1)
    gathered = lax.all_to_all(solution, "quad", split_axis=3, concat_axis=0, tiled=True)
    all_angles = 2.0 * math.pi * (jnp.arange(gathered.shape[0]).astype(jnp.float32) + 0.5) / QPTS
    return moment_terms(gathered, all_angles, radius[0])


def solution(mesh):
    in_specs = (P(None, None, "py", "pz"), P(None, None, "py", "pz"), P(None, "py", "pz"), P(), P())
    out_specs = P(None, None, None, "quad", "py", "pz")
    return jax.shard_map(
        per_device, mesh=mesh, in_specs=in_specs, out_specs=out_specs, check_vma=False
    )
```

profile of v0, /device:TPU:33, one launch (start us, length us, event | category | flops | bytes accessed | tf_op | source)
XLA Modules:
  0.0 176.5 jit_solution(8085165533482283820)
XLA Ops:
  0.0 1.3 pad_maximum_fusion.5
  2.5 1.9 %collective-permute-start.1 = (f32[1,2,4,16,4,128]{5,3,4,2,1,0:T(8,128)}, f32[1,2,4,16,4,128]{5,3,4,2,1,0:T(8,128)S(1)}, u32[]{:S(2)}, u32[]{:S(2)}) collective-permute-start(f32[1,2,4,16,4,128]{5,3,4,2,1,0:T(8,128)} %get-tuple-element.79), channel_id=1, source_target_pairs={{0,4},{4,8},{8,12},{12,16},{16,20},{20,24},{24,28},{28,0},{1,5},{5... | collective-permute-start | bytes 786440 | tf_op jit(solution)/shard_map/ppermute | solution.py:20
  4.7 1.6 copy.158
  6.7 1.6 copy.160
  8.3 1.3 collective-permute-start.3
  11.4 1.3 copy.156
  12.7 1.3 copy.150
  14.0 1.2 copy.151
  15.3 1.2 copy.163
  26.5 1.8 copy.222
  28.3 1.8 copy.223
  31.2 3.6 %select_maximum_fusion.3 = (f32[1,2,4,16,24,132]{5,4,3,2,1,0:T(8,128)S(1)}, f32[1,2,4,16,24,132]{5,4,3,2,1,0:T(8,128)S(1)}) fusion(f32[1,2,4,16,16,4]{5,4,3,2,1,0:T(8,128)S(1)} %copy.222, f32[1,2,4,16,4,128]{5,4,3,2,1,0:T(4,128)S(1)} %copy.157, f32[1,2,4,16,16,128]{5,4,3,2,1,0:T(8,128)} %copy.156, f32[1,2,4,16,4,128]{5,4,3,2,1,0:T(4,128)S(1)} %copy.155, ...), kind=kLoop, calls=%fused_computation.45 | loop fusion | flops 4055040 | bytes 4882432 | tf_op jit(solution)/shard_map/concatenate | solution.py:27
  34.8 4.4 %fusion.6 = (f32[1,2,4,16,16,128]{5,3,4,2,1,0:T(8,128)}, f32[1,2,4,16,16,128]{5,3,4,2,1,0:T(8,128)}, f32[1,2,4,16,16,128]{5,3,4,2,1,0:T(8,128)}, f32[1,2,4,16,16...) fusion(f32[1,2,4,16,16,128]{5,3,4,2,1,0:T(8,128)S(1)} %bitcast., ...), kind=kLoop, calls=%fused_computation.69 | loop fusion | flops 2097152 | bytes 9961472 | tf_op jit(solution)/shard_map/concatenate | solution.py:27
  39.2 10.0 %fusion.23 = f32[1,2,4,16,16,128]{5,4,3,2,1,0:T(8,128)S(1)} fusion(f32[1,2,4,16,24,132]{5,4,3,2,1,0:T(8,128)S(1)} %get-tuple-element.26, f32[1,2,4,16,24,132]{5,4,3,2,1,0:T(8,128)S(1)} %get-tuple-element.25, f32[1,2,4,15,16,128]{5,4,3,2,1,0:T(8,128)} %copy.150, f32[1,2,4,1,16,128]{5,4,3,2,1,0:T(8,128)} %bitcast.138, f32[1,2,4,1,16,128]{5,4,3,2,1,0:T(8,128)} %bitcast.137, ...), kind=kLoop, calls=%fused_computation.103 | loop fusion | flops 10747904 | bytes 27394048 | tf_op jit(solution)/shard_map/add | solution.py:71
  50.3 11.2 %all-to-all-start = ((f32[32,1,16]{2,1,0:T(1,128)}), f32[32,1,16]{2,1,0:T(1,128)S(1)}, u32[]{:S(2)}, u32[]{:S(2)}) async-start(f32[32,1,16]{2,1,0:T(1,128)} %broadcast_in_dim.7), calls=%async_computation | async-start | bytes 32768 | tf_op jit(solution)/shard_map/all_to_all | solution.py:34
  63.0 4.6 %all-to-all-done = f32[32,1,16]{2,1,0:T(1,128)S(1)} async-done(((f32[32,1,16]{2,1,0:T(1,128)}), f32[32,1,16]{2,1,0:T(1,128)S(1)}, u32[]{:S(2)}, u32[]{:S(2)}) %all-to-all-start) | async-done | bytes 2080 | tf_op jit(solution)/shard_map/all_to_all | solution.py:34
  69.6 1.3 fusion.43
  71.6 1.5 fusion.41
  73.1 1.5 fusion.39
  74.7 1.3 fusion.8
  79.3 2.8 %copy.216 = f32[1,2,4,16,16,4]{4,3,5,2,1,0:T(8,128)} copy(f32[1,2,4,16,16,4]{5,4,3,2,1,0:T(8,128)} %get-tuple-element.53) | data formatting | bytes 65536
  83.2 1.6 copy.217
  85.1 1.4 fusion.45
  87.2 3.6 %collective-permute-done.6 = f32[1,2,4,16,16,4]{4,3,5,2,1,0:T(8,128)} collective-permute-done((f32[1,2,4,16,16,4]{4,3,5,2,1,0:T(8,128)}, f32[1,2,4,16,16,4]{4,3,5,2,1,0:T(8,128)}, u32[]{:S(2)}, u32[]{:S(2)}) %collective-permute-start.6) | collective-permute-done | bytes 32800 | tf_op jit(solution)/shard_map/ppermute | solution.py:21
  90.7 1.8 copy.224
  92.5 3.9 %collective-permute-done.7 = f32[1,2,4,16,16,4]{4,3,5,2,1,0:T(8,128)} collective-permute-done((f32[1,2,4,16,16,4]{4,3,5,2,1,0:T(8,128)}, f32[1,2,4,16,16,4]{4,3,5,2,1,0:T(8,128)}, u32[]{:S(2)}, u32[]{:S(2)}) %collective-permute-start.7) | collective-permute-done | bytes 32800 | tf_op jit(solution)/shard_map/ppermute | solution.py:20
  96.4 2.7 %copy.225 = f32[1,2,4,16,16,4]{5,4,3,2,1,0:T(8,128)} copy(f32[1,2,4,16,16,4]{4,3,5,2,1,0:T(8,128)} %collective-permute-done.7) | data formatting | bytes 65536
  101.7 4.0 %select_maximum_fusion.1 = (f32[1,2,4,16,24,132]{5,4,3,2,1,0:T(8,128)}, f32[1,2,4,16,24,132]{5,4,3,2,1,0:T(8,128)}) fusion(f32[1,2,4,16,16,4]{5,4,3,2,1,0:T(8,128)S(1)} %copy.224, f32[1,2,4,16,4,128]{5,4,3,2,1,0:T(4,128)S(1)} %copy.182, f32[1,1,4,16,16,128]{5,4,3,2,1,0:T(8,128)S(1)} %bitcast.126, f32[1,1,4,16,16,128]{5,4,3,2,1,0:T(8,128)S(1)} %bitcast.113, ...), kind=kLoop, calls=%fused_computation.42 | loop fusion | flops 4866048 | bytes 4882432 | tf_op jit(solution)/shard_map/concatenate | solution.py:27
  105.7 12.7 %fusion.13 = f32[1,2,4,16,16,128]{5,4,3,2,1,0:T(8,128)S(1)} fusion(f32[1,2,4,16,24,132]{5,4,3,2,1,0:T(8,128)} %get-tuple-element.24, f32[1,2,4,16,24,132]{5,4,3,2,1,0:T(8,128)} %get-tuple-element.23, f32[1,2,4,16,20,128]{5,4,3,2,1,0:T(8,128)S(1)} %get-tuple-element.52, f32[1,2,4,16,20,128]{5,4,3,2,1,0:T(8,128)S(1)} %get-tuple-element.51, ...), kind=kLoop, calls=%fused_computation.77 | loop fusion | flops 10747904 | bytes 27394048 | tf_op jit(solution)/shard_map/add | solution.py:71
  119.0 11.9 %all_to_all.30 = f32[32,1,16]{2,1,0:T(1,128)S(1)} all-to-all(f32[32,1,16]{2,1,0:T(1,128)S(1)} %broadcast_in_dim.8), channel_id=1, replica_groups=mesh['quad'=8,'py'=8,'pz'=4] {'py','pz'}, dimensions={0} | all-to-all | bytes 4096 | tf_op jit(solution)/shard_map/all_to_all | solution.py:34
  132.9 7.9 %all-to-all-start.2 = ((f32[1,2,4,16,16,128]{5,4,2,1,0,3:T(8,128)}), f32[1,2,4,16,16,128]{5,4,2,1,0,3:T(8,128)S(1)}, u32[]{:S(2)}, u32[]{:S(2)}) async-start(f32[1,2,4,16,16,128]{5,4,2,1,0,3:T(8,128)} %copy.192), calls=%async_computation.2 | async-start | bytes 2097152 | tf_op jit(solution)/shard_map/all_to_all | solution.py:155
  140.9 31.3 %all-to-all-done.2 = f32[1,2,4,16,16,128]{5,4,2,1,0,3:T(8,128)S(1)} async-done(((f32[1,2,4,16,16,128]{5,4,2,1,0,3:T(8,128)}), f32[1,2,4,16,16,128]{5,4,2,1,0,3:T(8,128)S(1)}, u32[]{:S(2)}, u32[]{:S(2)}) %all-to-all-start.2) | async-done | bytes 1048608 | tf_op jit(solution)/shard_map/all_to_all | solution.py:155
  (79 shorter events, 33.5 us)
Async XLA Ops:
  2.5 27.6 %collective-permute-start.1 = (f32[1,2,4,16,4,128]{5,3,4,2,1,0:T(8,128)}, f32[1,2,4,16,4,128]{5,3,4,2,1,0:T(8,128)S(1)}, u32[]{:S(2)}, u32[]{:S(2)}) collective-permute-start(f32[1,2,4,16,4,128]{5,3,4,2,1,0:T(8,128)} %get-tuple-element.79), channel_id=1, source_target_pairs={{0,4},{4,8},{8,12},{12,16},{16,20},{20,24},{24,28},{28,0},{1,5},{5... | collective-permute-start | bytes 786440 | tf_op jit(solution)/shard_map/ppermute | solution.py:20
  4.3 25.8 %collective-permute-start = (f32[1,2,4,16,4,128]{5,3,4,2,1,0:T(8,128)}, f32[1,2,4,16,4,128]{5,3,4,2,1,0:T(8,128)}, u32[]{:S(2)}, u32[]{:S(2)}) collective-permute-start(f32[1,2,4,16,4,128]{5,3,4,2,1,0:T(8,128)} %get-tuple-element.80), channel_id=1, source_target_pairs={{4,0},{8,4},{12,8},{16,12},{20,16},{24,20},{28,24},{0,28},{5,1},{9... | collective-permute-start | bytes 786440 | tf_op jit(solution)/shard_map/ppermute | solution.py:21
  6.3 20.2 %collective-permute-start.2 = (f32[1,2,4,16,16,4]{4,3,5,2,1,0:T(8,128)}, f32[1,2,4,16,16,4]{4,3,5,2,1,0:T(8,128)}, u32[]{:S(2)}, u32[]{:S(2)}) collective-permute-start(f32[1,2,4,16,16,4]{4,3,5,2,1,0:T(8,128)} %copy.158), channel_id=1, source_target_pairs={{1,0},{2,1},{3,2},{0,3},{5,4},{6,5},{7,6},{4,7},{9,8},{10,9},{11,1... | collective-permute-start | bytes 98312 | tf_op jit(solution)/shard_map/ppermute | solution.py:21
  8.3 19.9 %collective-permute-start.3 = (f32[1,2,4,16,16,4]{4,3,5,2,1,0:T(8,128)}, f32[1,2,4,16,16,4]{4,3,5,2,1,0:T(8,128)}, u32[]{:S(2)}, u32[]{:S(2)}) collective-permute-start(f32[1,2,4,16,16,4]{4,3,5,2,1,0:T(8,128)} %copy.160), channel_id=1, source_target_pairs={{0,1},{1,2},{2,3},{3,0},{4,5},{5,6},{6,7},{7,4},{8,9},{9,10},{10,1... | collective-permute-start | bytes 98312 | tf_op jit(solution)/shard_map/ppermute | solution.py:20
  34.8 4.4 %copy-start = (f32[4,16,16,128]{3,2,1,0:T(8,128)S(1)}, f32[4,16,16,128]{3,2,1,0:T(8,128)}, u32[]{:S(2)}) copy-start(f32[4,16,16,128]{3,2,1,0:T(8,128)} %param.5) | copy-start | bytes 1572868
  34.8 4.4 %copy-start.1 = (f32[4,16,16,128]{3,2,1,0:T(8,128)S(1)}, f32[4,16,16,128]{3,2,1,0:T(8,128)}, u32[]{:S(2)}) copy-start(f32[4,16,16,128]{3,2,1,0:T(8,128)} %param.6) | copy-start | bytes 1572868
  34.8 4.4 %copy-start.3 = (f32[16,16,128]{2,1,0:T(8,128)S(1)}, f32[16,16,128]{2,1,0:T(8,128)}, u32[]{:S(2)}) copy-start(f32[16,16,128]{2,1,0:T(8,128)} %param.7) | copy-start | bytes 393220
  50.3 17.3 %all-to-all-start = ((f32[32,1,16]{2,1,0:T(1,128)}), f32[32,1,16]{2,1,0:T(1,128)S(1)}, u32[]{:S(2)}, u32[]{:S(2)}) async-start(f32[32,1,16]{2,1,0:T(1,128)} %broadcast_in_dim.7), calls=%async_computation | async-start | bytes 32768 | tf_op jit(solution)/shard_map/all_to_all | solution.py:34
  76.8 22.3 %collective-permute-start.4 = (f32[1,2,4,16,4,128]{5,3,4,2,1,0:T(8,128)}, f32[1,2,4,16,4,128]{5,3,4,2,1,0:T(8,128)}, u32[]{:S(2)}, u32[]{:S(2)}) collective-permute-start(f32[1,2,4,16,4,128]{5,3,4,2,1,0:T(8,128)} %copy.214), channel_id=1, source_target_pairs={{4,0},{8,4},{12,8},{16,12},{20,16},{24,20},{28,24},{0,28},{5,1},{9... | collective-permute-start | bytes 786440 | tf_op jit(solution)/shard_map/ppermute | solution.py:21
  78.1 22.1 %collective-permute-start.5 = (f32[1,2,4,16,4,128]{5,3,4,2,1,0:T(8,128)}, f32[1,2,4,16,4,128]{5,3,4,2,1,0:T(8,128)}, u32[]{:S(2)}, u32[]{:S(2)}) collective-permute-start(f32[1,2,4,16,4,128]{5,3,4,2,1,0:T(8,128)} %copy.215), channel_id=1, source_target_pairs={{0,4},{4,8},{8,12},{12,16},{16,20},{20,24},{24,28},{28,0},{1,5},{5... | collective-permute-start | bytes 786440 | tf_op jit(solution)/shard_map/ppermute | solution.py:20
  82.1 8.6 %collective-permute-start.6 = (f32[1,2,4,16,16,4]{4,3,5,2,1,0:T(8,128)}, f32[1,2,4,16,16,4]{4,3,5,2,1,0:T(8,128)}, u32[]{:S(2)}, u32[]{:S(2)}) collective-permute-start(f32[1,2,4,16,16,4]{4,3,5,2,1,0:T(8,128)} %copy.216), channel_id=1, source_target_pairs={{1,0},{2,1},{3,2},{0,3},{5,4},{6,5},{7,6},{4,7},{9,8},{10,9},{11,1... | collective-permute-start | bytes 98312 | tf_op jit(solution)/shard_map/ppermute | solution.py:21
  84.8 11.6 %collective-permute-start.7 = (f32[1,2,4,16,16,4]{4,3,5,2,1,0:T(8,128)}, f32[1,2,4,16,16,4]{4,3,5,2,1,0:T(8,128)}, u32[]{:S(2)}, u32[]{:S(2)}) collective-permute-start(f32[1,2,4,16,16,4]{4,3,5,2,1,0:T(8,128)} %copy.217), channel_id=1, source_target_pairs={{0,1},{1,2},{2,3},{3,0},{4,5},{5,6},{6,7},{7,4},{8,9},{9,10},{10,1... | collective-permute-start | bytes 98312 | tf_op jit(solution)/shard_map/ppermute | solution.py:20
  99.1 2.6 %copy-start.2 = (f32[1,2,4,16,16,4]{5,4,3,2,1,0:T(8,128)S(1)}, f32[1,2,4,16,16,4]{5,4,3,2,1,0:T(8,128)}, u32[]{:S(2)}) copy-start(f32[1,2,4,16,16,4]{5,4,3,2,1,0:T(8,128)} %copy.225) | copy-start | bytes 98308
  132.9 39.3 %all-to-all-start.2 = ((f32[1,2,4,16,16,128]{5,4,2,1,0,3:T(8,128)}), f32[1,2,4,16,16,128]{5,4,2,1,0,3:T(8,128)S(1)}, u32[]{:S(2)}, u32[]{:S(2)}) async-start(f32[1,2,4,16,16,128]{5,4,2,1,0,3:T(8,128)} %copy.192), calls=%async_computation.2 | async-start | bytes 2097152 | tf_op jit(solution)/shard_map/all_to_all | solution.py:155
where the time goes:
time: 177 us
  other arithmetic  48.8 us (28%)
  waiting for transfers between devices  43.3 us (24%)
  local copies, waits for them, and re-layouts  42.1 us (24%)
  starting transfers between devices  25.8 us (15%)
  blocking collectives  11.9 us (7%)
  matrix products  2.71 us (2%)
    all_to_all x1, waiting for transfers between devices, per_device(): lax.all_to_all(solution, 'quad', split_axis=3, concat_axis=0, tiled=True)  31.3 us
    add x2, other arithmetic, apply_operator(): return -0.5 * laplace + potential * field  22.7 us
    slice x22, local copies, waits for them, and re-layouts, apply_operator(): beside_all = jnp.roll(field, offset, 3) + jnp.roll(field, -offset, 3)  15.5 us
    unnamed x16, local copies, waits for them, and re-layouts  13.9 us
    concatenate x4, other arithmetic, with_halo(): jnp.concatenate([jnp.pad(low, around), value, jnp.pad(high, around)], axi...  12.3 us
    all_to_all x1, blocking collectives, sent_to_all(): lax.all_to_all(jnp.broadcast_to(value[None], (count, *value.shape)), axis...  11.9 us
    all_to_all x1, starting transfers between devices, sent_to_all(): lax.all_to_all(jnp.broadcast_to(value[None], (count, *value.shape)), axis...  11.2 us
    another operation x10, other arithmetic, per_device(): hres = apply_operator(jnp.stack(residual, 1), potential)  10.1 us
  transfers between devices with their start and end apart: 10, of which 4 were waited for; matrix products, arithmetic and copies ran while one was open for 21% of the time, Pallas kernels for 0%

commit v1 on v0

--- a/solution.py
+++ b/solution.py
@@ -7,6 +7,13 @@
 QPTS = 8
 MOMS = 4
 stencil_weights = (-205.0 / 72.0, 8.0 / 5.0, -1.0 / 5.0, 8.0 / 315.0, -1.0 / 560.0)
+
+
+def swap_blocks(block, axis, split, join):
+    size = lax.axis_size(axis)
+    parts = jnp.stack(jnp.split(block, size, axis=split), axis=0)
+    parts = lax.all_to_all(parts, axis, split_axis=0, concat_axis=0)
+    return jnp.concatenate(parts, axis=join)
 
 
 def with_halo(value, sides, width):
@@ -152,7 +159,7 @@
     alpha_next = complex_div(rho_next, curv_next)
     step_part = complex_mul(spread(alpha_next), direction)
     solution = jnp.stack((first_iterate[0] + step_part[0], first_iterate[1] + step_part[1]), 1)
-    gathered = lax.all_to_all(solution, "quad", split_axis=3, concat_axis=0, tiled=True)
+    gathered = swap_blocks(solution, "quad", 3, 0)
     all_angles = 2.0 * math.pi * (jnp.arange(gathered.shape[0]).astype(jnp.float32) + 0.5) / QPTS
     return moment_terms(gathered, all_angles, radius[0])
 

time: 177 us -> 181 us (1.023)
  other arithmetic: 48.8 us -> 54 us
    unnamed x0 -> x7, other arithmetic: none -> 4.6 us
  transfers between devices with their start and end apart: 10 -> 10, of which waited for: 4 -> 4; matrix products, arithmetic and copies ran while one was open for 21% -> 20% of each run, Pallas kernels for 0% -> 0%
where the time goes in v1:
time: 181 us
  other arithmetic  54 us (30%)
  waiting for transfers between devices  43.3 us (24%)
  local copies, waits for them, and re-layouts  41 us (23%)
  starting transfers between devices  25.8 us (14%)
  blocking collectives  11.9 us (7%)
  matrix products  2.71 us (1%)
    all_to_all x1, waiting for transfers between devices, swap_blocks(): parts = lax.all_to_all(parts, axis, split_axis=0, concat_axis=0)  31.3 us
    add x2, other arithmetic, apply_operator(): return -0.5 * laplace + potential * field  22.7 us
    slice x22, local copies, waits for them, and re-layouts, apply_operator(): beside_all = jnp.roll(field, offset, 3) + jnp.roll(field, -offset, 3)  15.5 us
    unnamed x16, local copies, waits for them, and re-layouts  13.9 us
    concatenate x4, other arithmetic, with_halo(): jnp.concatenate([jnp.pad(low, around), value, jnp.pad(high, around)], axi...  12.3 us
    all_to_all x1, blocking collectives, sent_to_all(): lax.all_to_all(jnp.broadcast_to(value[None], (count, *value.shape)), axis...  11.9 us
    all_to_all x1, starting transfers between devices, sent_to_all(): lax.all_to_all(jnp.broadcast_to(value[None], (count, *value.shape)), axis...  11.2 us
    another operation x10, other arithmetic, per_device(): hres = apply_operator(jnp.stack(residual, 1), potential)  10.1 us
  transfers between devices with their start and end apart: 10, of which 4 were waited for; matrix products, arithmetic and copies ran while one was open for 20% of the time, Pallas kernels for 0%

profile of v1, /device:TPU:33, one launch (start us, length us, event | category | flops | bytes accessed | tf_op | source)
XLA Modules:
  0.0 180.6 jit_solution(8539376305006599491)
XLA Ops:
  0.0 1.3 pad_maximum_fusion.5
  2.5 1.9 %collective-permute-start.1 = (f32[1,2,4,16,4,128]{5,3,4,2,1,0:T(8,128)}, f32[1,2,4,16,4,128]{5,3,4,2,1,0:T(8,128)S(1)}, u32[]{:S(2)}, u32[]{:S(2)}) collective-permute-start(f32[1,2,4,16,4,128]{5,3,4,2,1,0:T(8,128)} %get-tuple-element.79), channel_id=1, source_target_pairs={{0,4},{4,8},{8,12},{12,16},{16,20},{20,24},{24,28},{28,0},{1,5},{5... | collective-permute-start | bytes 786440 | tf_op jit(solution)/shard_map/ppermute | solution.py:27
  4.7 1.6 copy.158
  6.7 1.6 copy.160
  8.3 1.3 collective-permute-start.3
  11.4 1.3 copy.156
  12.7 1.3 copy.150
  14.0 1.2 copy.151
  15.3 1.2 copy.163
  26.5 1.8 copy.218
  28.3 1.8 copy.219
  31.2 3.6 %select_maximum_fusion.3 = (f32[1,2,4,16,24,132]{5,4,3,2,1,0:T(8,128)S(1)}, f32[1,2,4,16,24,132]{5,4,3,2,1,0:T(8,128)S(1)}) fusion(f32[1,2,4,16,16,4]{5,4,3,2,1,0:T(8,128)S(1)} %copy.218, f32[1,2,4,16,4,128]{5,4,3,2,1,0:T(4,128)S(1)} %copy.157, f32[1,2,4,16,16,128]{5,4,3,2,1,0:T(8,128)} %copy.156, f32[1,2,4,16,4,128]{5,4,3,2,1,0:T(4,128)S(1)} %copy.155, ...), kind=kLoop, calls=%fused_computation.45 | loop fusion | flops 4055040 | bytes 4882432 | tf_op jit(solution)/shard_map/concatenate | solution.py:34
  34.8 4.4 %fusion.6 = (f32[1,2,4,16,16,128]{5,3,4,2,1,0:T(8,128)}, f32[1,2,4,16,16,128]{5,3,4,2,1,0:T(8,128)}, f32[1,2,4,16,16,128]{5,3,4,2,1,0:T(8,128)}, f32[1,2,4,16,16...) fusion(f32[1,2,4,16,16,128]{5,3,4,2,1,0:T(8,128)S(1)} %bitcast., ...), kind=kLoop, calls=%fused_computation.83 | loop fusion | flops 2097152 | bytes 9961472 | tf_op jit(solution)/shard_map/concatenate | solution.py:34
  39.2 10.0 %fusion.23 = f32[1,2,4,16,16,128]{5,4,3,2,1,0:T(8,128)S(1)} fusion(f32[1,2,4,16,24,132]{5,4,3,2,1,0:T(8,128)S(1)} %get-tuple-element.26, f32[1,2,4,16,24,132]{5,4,3,2,1,0:T(8,128)S(1)} %get-tuple-element.25, f32[1,2,4,15,16,128]{5,4,3,2,1,0:T(8,128)} %copy.150, f32[1,2,4,1,16,128]{5,4,3,2,1,0:T(8,128)} %bitcast.166, f32[1,2,4,1,16,128]{5,4,3,2,1,0:T(8,128)} %bitcast.165, ...), kind=kLoop, calls=%fused_computation.117 | loop fusion | flops 10747904 | bytes 27394048 | tf_op jit(solution)/shard_map/add | solution.py:78
  50.3 11.2 %all-to-all-start = ((f32[32,1,16]{2,1,0:T(1,128)}), f32[32,1,16]{2,1,0:T(1,128)S(1)}, u32[]{:S(2)}, u32[]{:S(2)}) async-start(f32[32,1,16]{2,1,0:T(1,128)} %broadcast_in_dim.7), calls=%async_computation | async-start | bytes 32768 | tf_op jit(solution)/shard_map/all_to_all | solution.py:41
  63.0 4.6 %all-to-all-done = f32[32,1,16]{2,1,0:T(1,128)S(1)} async-done(((f32[32,1,16]{2,1,0:T(1,128)}), f32[32,1,16]{2,1,0:T(1,128)S(1)}, u32[]{:S(2)}, u32[]{:S(2)}) %all-to-all-start) | async-done | bytes 2080 | tf_op jit(solution)/shard_map/all_to_all | solution.py:41
  69.6 1.3 fusion.43
  71.6 1.5 fusion.41
  73.1 1.5 fusion.39
  74.7 1.3 fusion.8
  79.3 2.8 %copy.212 = f32[1,2,4,16,16,4]{4,3,5,2,1,0:T(8,128)} copy(f32[1,2,4,16,16,4]{5,4,3,2,1,0:T(8,128)} %get-tuple-element.53) | data formatting | bytes 65536
  83.2 1.6 copy.213
  85.1 1.4 fusion.45
  87.2 3.6 %collective-permute-done.6 = f32[1,2,4,16,16,4]{4,3,5,2,1,0:T(8,128)} collective-permute-done((f32[1,2,4,16,16,4]{4,3,5,2,1,0:T(8,128)}, f32[1,2,4,16,16,4]{4,3,5,2,1,0:T(8,128)}, u32[]{:S(2)}, u32[]{:S(2)}) %collective-permute-start.6) | collective-permute-done | bytes 32800 | tf_op jit(solution)/shard_map/ppermute | solution.py:28
  90.7 1.8 copy.220
  92.5 3.9 %collective-permute-done.7 = f32[1,2,4,16,16,4]{4,3,5,2,1,0:T(8,128)} collective-permute-done((f32[1,2,4,16,16,4]{4,3,5,2,1,0:T(8,128)}, f32[1,2,4,16,16,4]{4,3,5,2,1,0:T(8,128)}, u32[]{:S(2)}, u32[]{:S(2)}) %collective-permute-start.7) | collective-permute-done | bytes 32800 | tf_op jit(solution)/shard_map/ppermute | solution.py:27
  96.4 2.7 %copy.221 = f32[1,2,4,16,16,4]{5,4,3,2,1,0:T(8,128)} copy(f32[1,2,4,16,16,4]{4,3,5,2,1,0:T(8,128)} %collective-permute-done.7) | data formatting | bytes 65536
  101.7 4.0 %select_maximum_fusion.1 = (f32[1,2,4,16,24,132]{5,4,3,2,1,0:T(8,128)}, f32[1,2,4,16,24,132]{5,4,3,2,1,0:T(8,128)}) fusion(f32[1,2,4,16,16,4]{5,4,3,2,1,0:T(8,128)S(1)} %copy.220, f32[1,2,4,16,4,128]{5,4,3,2,1,0:T(4,128)S(1)} %copy.182, f32[1,1,4,16,16,128]{5,4,3,2,1,0:T(8,128)S(1)} %bitcast.155, f32[1,1,4,16,16,128]{5,4,3,2,1,0:T(8,128)S(1)} %bitcast.142, ...), kind=kLoop, calls=%fused_computation.42 | loop fusion | flops 4866048 | bytes 4882432 | tf_op jit(solution)/shard_map/concatenate | solution.py:34
  105.7 12.7 %fusion.13 = f32[1,2,4,16,16,128]{5,4,3,2,1,0:T(8,128)S(1)} fusion(f32[1,2,4,16,24,132]{5,4,3,2,1,0:T(8,128)} %get-tuple-element.24, f32[1,2,4,16,24,132]{5,4,3,2,1,0:T(8,128)} %get-tuple-element.23, f32[1,2,4,16,20,128]{5,4,3,2,1,0:T(8,128)S(1)} %get-tuple-element.52, f32[1,2,4,16,20,128]{5,4,3,2,1,0:T(8,128)S(1)} %get-tuple-element.51, ...), kind=kLoop, calls=%fused_computation.91 | loop fusion | flops 10747904 | bytes 27394048 | tf_op jit(solution)/shard_map/add | solution.py:78
  119.0 11.9 %all_to_all.17 = f32[32,1,16]{2,1,0:T(1,128)S(1)} all-to-all(f32[32,1,16]{2,1,0:T(1,128)S(1)} %broadcast_in_dim.8), channel_id=1, replica_groups=mesh['quad'=8,'py'=8,'pz'=4] {'py','pz'}, dimensions={0} | all-to-all | bytes 4096 | tf_op jit(solution)/shard_map/all_to_all | solution.py:41
  137.0 7.9 %all-to-all-start.2 = ((f32[8,1,2,4,2,16,128]{6,5,4,3,2,1,0:T(8,128)}), f32[8,1,2,4,2,16,128]{6,5,4,3,2,1,0:T(8,128)S(1)}, u32[]{:S(2)}, u32[]{:S(2)}) async-start(f32[8,1,2,4,2,16,128]{6,5,4,3,2,1,0:T(8,128)} %fusion.80), calls=%async_computation.2 | async-start | bytes 2097152 | tf_op jit(solution)/shard_map/all_to_all | solution.py:15
  144.9 31.3 %all-to-all-done.2 = f32[8,1,2,4,2,16,128]{6,5,4,3,2,1,0:T(8,128)S(1)} async-done(((f32[8,1,2,4,2,16,128]{6,5,4,3,2,1,0:T(8,128)}), f32[8,1,2,4,2,16,128]{6,5,4,3,2,1,0:T(8,128)S(1)}, u32[]{:S(2)}, u32[]{:S(2)}) %all-to-all-start.2) | async-done | bytes 1048608 | tf_op jit(solution)/shard_map/all_to_all | solution.py:15
  (85 shorter events, 37.6 us)
Async XLA Ops:
  2.5 27.6 %collective-permute-start.1 = (f32[1,2,4,16,4,128]{5,3,4,2,1,0:T(8,128)}, f32[1,2,4,16,4,128]{5,3,4,2,1,0:T(8,128)S(1)}, u32[]{:S(2)}, u32[]{:S(2)}) collective-permute-start(f32[1,2,4,16,4,128]{5,3,4,2,1,0:T(8,128)} %get-tuple-element.79), channel_id=1, source_target_pairs={{0,4},{4,8},{8,12},{12,16},{16,20},{20,24},{24,28},{28,0},{1,5},{5... | collective-permute-start | bytes 786440 | tf_op jit(solution)/shard_map/ppermute | solution.py:27
  4.3 25.8 %collective-permute-start = (f32[1,2,4,16,4,128]{5,3,4,2,1,0:T(8,128)}, f32[1,2,4,16,4,128]{5,3,4,2,1,0:T(8,128)}, u32[]{:S(2)}, u32[]{:S(2)}) collective-permute-start(f32[1,2,4,16,4,128]{5,3,4,2,1,0:T(8,128)} %get-tuple-element.80), channel_id=1, source_target_pairs={{4,0},{8,4},{12,8},{16,12},{20,16},{24,20},{28,24},{0,28},{5,1},{9... | collective-permute-start | bytes 786440 | tf_op jit(solution)/shard_map/ppermute | solution.py:28
  6.3 20.2 %collective-permute-start.2 = (f32[1,2,4,16,16,4]{4,3,5,2,1,0:T(8,128)}, f32[1,2,4,16,16,4]{4,3,5,2,1,0:T(8,128)}, u32[]{:S(2)}, u32[]{:S(2)}) collective-permute-start(f32[1,2,4,16,16,4]{4,3,5,2,1,0:T(8,128)} %copy.158), channel_id=1, source_target_pairs={{1,0},{2,1},{3,2},{0,3},{5,4},{6,5},{7,6},{4,7},{9,8},{10,9},{11,1... | collective-permute-start | bytes 98312 | tf_op jit(solution)/shard_map/ppermute | solution.py:28
  8.3 19.9 %collective-permute-start.3 = (f32[1,2,4,16,16,4]{4,3,5,2,1,0:T(8,128)}, f32[1,2,4,16,16,4]{4,3,5,2,1,0:T(8,128)}, u32[]{:S(2)}, u32[]{:S(2)}) collective-permute-start(f32[1,2,4,16,16,4]{4,3,5,2,1,0:T(8,128)} %copy.160), channel_id=1, source_target_pairs={{0,1},{1,2},{2,3},{3,0},{4,5},{5,6},{6,7},{7,4},{8,9},{9,10},{10,1... | collective-permute-start | bytes 98312 | tf_op jit(solution)/shard_map/ppermute | solution.py:27
  34.8 4.4 %copy-start = (f32[4,16,16,128]{3,2,1,0:T(8,128)S(1)}, f32[4,16,16,128]{3,2,1,0:T(8,128)}, u32[]{:S(2)}) copy-start(f32[4,16,16,128]{3,2,1,0:T(8,128)} %param.5) | copy-start | bytes 1572868
  34.8 4.4 %copy-start.1 = (f32[4,16,16,128]{3,2,1,0:T(8,128)S(1)}, f32[4,16,16,128]{3,2,1,0:T(8,128)}, u32[]{:S(2)}) copy-start(f32[4,16,16,128]{3,2,1,0:T(8,128)} %param.6) | copy-start | bytes 1572868
  34.8 4.4 %copy-start.3 = (f32[16,16,128]{2,1,0:T(8,128)S(1)}, f32[16,16,128]{2,1,0:T(8,128)}, u32[]{:S(2)}) copy-start(f32[16,16,128]{2,1,0:T(8,128)} %param.7) | copy-start | bytes 393220
  50.3 17.3 %all-to-all-start = ((f32[32,1,16]{2,1,0:T(1,128)}), f32[32,1,16]{2,1,0:T(1,128)S(1)}, u32[]{:S(2)}, u32[]{:S(2)}) async-start(f32[32,1,16]{2,1,0:T(1,128)} %broadcast_in_dim.7), calls=%async_computation | async-start | bytes 32768 | tf_op jit(solution)/shard_map/all_to_all | solution.py:41
  76.8 22.3 %collective-permute-start.4 = (f32[1,2,4,16,4,128]{5,3,4,2,1,0:T(8,128)}, f32[1,2,4,16,4,128]{5,3,4,2,1,0:T(8,128)}, u32[]{:S(2)}, u32[]{:S(2)}) collective-permute-start(f32[1,2,4,16,4,128]{5,3,4,2,1,0:T(8,128)} %copy.210), channel_id=1, source_target_pairs={{4,0},{8,4},{12,8},{16,12},{20,16},{24,20},{28,24},{0,28},{5,1},{9... | collective-permute-start | bytes 786440 | tf_op jit(solution)/shard_map/ppermute | solution.py:28
  78.1 22.1 %collective-permute-start.5 = (f32[1,2,4,16,4,128]{5,3,4,2,1,0:T(8,128)}, f32[1,2,4,16,4,128]{5,3,4,2,1,0:T(8,128)}, u32[]{:S(2)}, u32[]{:S(2)}) collective-permute-start(f32[1,2,4,16,4,128]{5,3,4,2,1,0:T(8,128)} %copy.211), channel_id=1, source_target_pairs={{0,4},{4,8},{8,12},{12,16},{16,20},{20,24},{24,28},{28,0},{1,5},{5... | collective-permute-start | bytes 786440 | tf_op jit(solution)/shard_map/ppermute | solution.py:27
  82.1 8.6 %collective-permute-start.6 = (f32[1,2,4,16,16,4]{4,3,5,2,1,0:T(8,128)}, f32[1,2,4,16,16,4]{4,3,5,2,1,0:T(8,128)}, u32[]{:S(2)}, u32[]{:S(2)}) collective-permute-start(f32[1,2,4,16,16,4]{4,3,5,2,1,0:T(8,128)} %copy.212), channel_id=1, source_target_pairs={{1,0},{2,1},{3,2},{0,3},{5,4},{6,5},{7,6},{4,7},{9,8},{10,9},{11,1... | collective-permute-start | bytes 98312 | tf_op jit(solution)/shard_map/ppermute | solution.py:28
  84.8 11.6 %collective-permute-start.7 = (f32[1,2,4,16,16,4]{4,3,5,2,1,0:T(8,128)}, f32[1,2,4,16,16,4]{4,3,5,2,1,0:T(8,128)}, u32[]{:S(2)}, u32[]{:S(2)}) collective-permute-start(f32[1,2,4,16,16,4]{4,3,5,2,1,0:T(8,128)} %copy.213), channel_id=1, source_target_pairs={{0,1},{1,2},{2,3},{3,0},{4,5},{5,6},{6,7},{7,4},{8,9},{9,10},{10,1... | collective-permute-start | bytes 98312 | tf_op jit(solution)/shard_map/ppermute | solution.py:27
  99.1 2.6 %copy-start.2 = (f32[1,2,4,16,16,4]{5,4,3,2,1,0:T(8,128)S(1)}, f32[1,2,4,16,16,4]{5,4,3,2,1,0:T(8,128)}, u32[]{:S(2)}) copy-start(f32[1,2,4,16,16,4]{5,4,3,2,1,0:T(8,128)} %copy.221) | copy-start | bytes 98308
  137.0 39.3 %all-to-all-start.2 = ((f32[8,1,2,4,2,16,128]{6,5,4,3,2,1,0:T(8,128)}), f32[8,1,2,4,2,16,128]{6,5,4,3,2,1,0:T(8,128)S(1)}, u32[]{:S(2)}, u32[]{:S(2)}) async-start(f32[8,1,2,4,2,16,128]{6,5,4,3,2,1,0:T(8,128)} %fusion.80), calls=%async_computation.2 | async-start | bytes 2097152 | tf_op jit(solution)/shard_map/all_to_all | solution.py:15
